TPU v7x, 32 devices: a whole 2x2x4 slice. The times are simulated.
32 devices in a mesh: ctx: 8 (over z, y), head: 2 (over core), pair: 2 (over x).
Axes of the slice: x: 2, y: 2, z: 4, core: 2. Of those that a mesh axis runs over, the one named last changes fastest.
Arguments:
- tokens_in: bfloat16 [2, 256, 2048], P(None, ('ctx', 'pair')), may hold values from -6 to 6
- attn_gain: float32 [2048], replicated, may hold values from 0.1 to 1.9
- query_matrix: bfloat16 [2048, 2048], P(None, ('head', 'pair')), may hold values from -20 to 20
- key_matrix: bfloat16 [256, 2048], P(('head', 'pair')), may hold values from -1 to 1
- value_matrix: bfloat16 [256, 2048], P(('head', 'pair')), may hold values from -0.125 to 0.125
- output_matrix: bfloat16 [2048, 2048], P(None, ('head', 'pair')), may hold values from -0.125 to 0.125
- moe_gain: float32 [2048], replicated, may hold values from 0.1 to 1.9
- chosen_experts: int32 [2, 256, 8], P('head', ('ctx', 'pair')), may hold values from 0 to 15, all different within a row; in each aligned block of 16 rows (0 to 15, 16 to 31, ..., all dimensions but the last counted through in order) at most 9 rows name the same one
- combine_weights: float32 [2, 256, 8], P('head', ('ctx', 'pair')), may hold values from 0.02 to 0.5
- gate_weight: bfloat16 [16, 768, 2048], P(('ctx', 'head'), 'pair'), may hold values from -0.125 to 0.125
- up_weight: bfloat16 [16, 768, 2048], P(('ctx', 'head'), 'pair'), may hold values from -0.125 to 0.125
- down_weight: bfloat16 [16, 768, 2048], P(('ctx', 'head'), 'pair'), may hold values from -0.21875 to 0.21875
Outputs:
- layer_out: bfloat16 [2, 256, 2048], P('head', ('ctx', 'pair'))
Inputs may be any that keep to these rules, and one draw needn't show every extreme that they name: `chosen_experts`: each token names 8 different experts; among the 16 tokens of one sequence that one device holds, no expert is named more than 9 times.
All inputs are finite; a program needn't handle non-finite values.
Results may differ from a plain program's by a relative error of at most 0.013.
Values may be sent and summed in bfloat16 or wider, within the bound.
A program may use at most 64 MiB of HBM per device.

v0:
```python
import jax
import jax.numpy as jnp
from jax import lax
from jax.sharding import PartitionSpec as P

ROPE_BASE = 1000000.0
EPSILON = 1e-06
MASKED = -1e30


def normalize(values, gain_vector):
    wide = values.astype(jnp.float32)
    mean_square = jnp.mean(wide * wide, axis=-1, keepdims=True)
    return (wide * lax.rsqrt(mean_square + EPSILON) * gain_vector).astype(jnp.bfloat16)


def rotate(values, positions):
    half_dim = values.shape[-1] // 2
    frequency = ROPE_BASE ** (-(jnp.arange(half_dim).astype(jnp.float32) * 2.0) / values.shape[-1])
    angles = positions[:, None] * frequency[None, :]
    cosine_part = jnp.cos(angles)[:, None, :]
    sine_part = jnp.sin(angles)[:, None, :]
    lower_half = values[..., :half_dim]
    upper_half = values[..., half_dim:]
    return jnp.concatenate(
        [
            lower_half * cosine_part - upper_half * sine_part,
            upper_half * cosine_part + lower_half * sine_part,
        ],
        axis=-1,
    )


def body(
    tokens_in,
    attn_gain,
    query_matrix,
    key_matrix,
    value_matrix,
    output_matrix,
    moe_gain,
    chosen_experts,
    combine_weights,
    gate_weight,
    up_weight,
    down_weight,
):
    pair_count = lax.axis_size("pair")
    head_count = lax.axis_size("head")
    ctx_count = lax.axis_size("ctx")
    seq_count, own_len, model_width = tokens_in.shape
    block_len = own_len * pair_count
    normalized_input = normalize(tokens_in, attn_gain)
    block_rows = lax.all_gather(normalized_input, "pair", axis=1, tiled=True)
    block_start = lax.axis_index("ctx") * block_len
    query_pos = block_start + jnp.arange(block_len)
    positions = query_pos.astype(jnp.float32)
    key_part = jnp.einsum("spd,hd->sph", block_rows, key_matrix, preferred_element_type=jnp.float32)
    value_part = jnp.einsum(
        "spd,hd->sph", block_rows, value_matrix, preferred_element_type=jnp.float32
    )
    key_full, value_full = (
        lax.all_gather(key_part.astype(jnp.bfloat16), "pair", axis=2, tiled=True).astype(
            key_part.dtype
        ),
        lax.all_gather(value_part.astype(jnp.bfloat16), "pair", axis=2, tiled=True).astype(
            value_part.dtype
        ),
    )
    head_dim = key_full.shape[2]
    local_heads = query_matrix.shape[1] // head_dim
    query_unrotated = jnp.einsum(
        "spd,dh->sph", block_rows, query_matrix, preferred_element_type=jnp.float32
    )
    queries = rotate(
        query_unrotated.reshape(seq_count, block_len, local_heads, head_dim), positions
    ).astype(jnp.bfloat16)
    rotated_keys = rotate(key_full.reshape(seq_count, block_len, 1, head_dim), positions)[
        :, :, 0
    ].astype(jnp.bfloat16)
    every_value_row = value_full.astype(jnp.bfloat16)
    scaling = head_dim ** (-0.5)
    last_query = block_start + block_len - 1
    start_state = (
        jnp.full((seq_count, block_len, local_heads), MASKED, jnp.float32),
        jnp.zeros((seq_count, block_len, local_heads), jnp.float32),
        jnp.zeros((seq_count, block_len, local_heads, head_dim), jnp.float32),
    )
    key_rows = lax.all_gather(rotated_keys, "ctx", axis=1, tiled=True)
    value_rows = lax.all_gather(every_value_row, "ctx", axis=1, tiled=True)
    key_span = key_rows.shape[1]

    def compute(running_state):
        row_peak, denominator, accumulated = running_state
        key_pos = jnp.arange(key_span)
        allowed = (key_pos[None, :] <= query_pos[:, None])[None, :, None, :]
        scores = (
            jnp.einsum("sphd,skd->sphk", queries, key_rows, preferred_element_type=jnp.float32)
            * scaling
        )
        scores = jnp.where(allowed, scores, MASKED)
        new_peak = jnp.maximum(row_peak, jnp.max(scores, axis=-1))
        weights = jnp.where(allowed, jnp.exp(scores - new_peak[..., None]), 0.0)
        denominator = jnp.sum(weights, axis=-1)
        accumulated = jnp.einsum(
            "sphk,skd->sphd",
            weights.astype(jnp.bfloat16),
            value_rows,
            preferred_element_type=jnp.float32,
        )
        return (new_peak, denominator, accumulated)

    row_peak, denominator, accumulated = lax.cond(
        jnp.int32(0) > last_query, lambda skipped: skipped, compute, start_state
    )
    attended = (
        (accumulated / denominator[..., None])
        .astype(jnp.bfloat16)
        .reshape(seq_count, block_len, local_heads * head_dim)
    )
    projected = jnp.einsum(
        "sph,hc->spc",
        lax.all_gather(attended, ("head", "pair"), axis=2, tiled=True),
        output_matrix,
        preferred_element_type=jnp.float32,
    )
    projected = projected.astype(jnp.bfloat16).reshape(
        seq_count * pair_count, own_len, output_matrix.shape[1]
    )
    owned_rows = lax.all_to_all(
        projected, ("head", "pair"), split_axis=0, concat_axis=2, tiled=True
    )[0]
    own_tokens = lax.dynamic_index_in_dim(tokens_in, lax.axis_index("head"), 0, keepdims=False)
    residual = (own_tokens.astype(jnp.float32) + owned_rows.astype(jnp.float32)).astype(
        jnp.bfloat16
    )
    moe_in = normalize(residual, moe_gain)
    expert_total = ctx_count * head_count
    top_count = chosen_experts.shape[-1]
    capacity = max(2, (own_len * top_count + expert_total - 1) // expert_total + 1)
    picked = chosen_experts.reshape(own_len, top_count)
    member = (picked[..., None] == jnp.arange(expert_total)[None, None, :]).astype(jnp.int32)
    running = jnp.cumsum(member.reshape(own_len * top_count, expert_total), axis=0).reshape(
        own_len, top_count, expert_total
    )
    slot_rank = jnp.sum((running - 1) * member, axis=-1)
    slot_ids = picked * capacity + slot_rank
    placing = jnp.any(
        slot_ids[..., None] == jnp.arange(expert_total * capacity)[None, None, :], axis=1
    ).astype(jnp.bfloat16)
    outgoing = jnp.einsum("ts,td->sd", placing, moe_in, preferred_element_type=jnp.float32).astype(
        jnp.bfloat16
    )
    incoming = lax.all_to_all(
        outgoing.reshape(expert_total, capacity, model_width),
        ("ctx", "head"),
        split_axis=0,
        concat_axis=0,
        tiled=True,
    )
    incoming = incoming.reshape(expert_total * capacity, model_width)
    slot_rows = incoming.shape[0]
    gate_local = gate_weight[0]
    up_local = up_weight[0]
    down_local = down_weight[0]
    quarter = gate_local.shape[0]
    totals = jnp.zeros((slot_rows, model_width), jnp.float32)
    gate_rows_w = lax.all_gather(gate_local, "pair", axis=0, tiled=True)
    up_rows_w = lax.all_gather(up_local, "pair", axis=0, tiled=True)
    down_rows_w = lax.all_gather(down_local, "pair", axis=0, tiled=True)
    for part_id in range(gate_rows_w.shape[0] // quarter):
        lower_row = part_id * quarter
        gate_part = lax.dot_general(
            gate_rows_w[lower_row : lower_row + quarter],
            incoming,
            (((1,), (1,)), ((), ())),
            preferred_element_type=jnp.float32,
        )
        up_part = lax.dot_general(
            up_rows_w[lower_row : lower_row + quarter],
            incoming,
            (((1,), (1,)), ((), ())),
            preferred_element_type=jnp.float32,
        )
        hidden = (jax.nn.silu(gate_part) * up_part).astype(jnp.bfloat16)
        partial_value = lax.dot_general(
            hidden,
            down_rows_w[lower_row : lower_row + quarter],
            (((0,), (0,)), ((), ())),
            preferred_element_type=jnp.float32,
        )
        totals = totals + lax.optimization_barrier(partial_value.astype(jnp.bfloat16)).astype(
            jnp.float32
        )
    expert_out = totals
    expert_out = expert_out.astype(jnp.bfloat16)
    returned = lax.all_to_all(
        expert_out.reshape(expert_total, capacity, model_width),
        ("ctx", "head"),
        split_axis=0,
        concat_axis=0,
        tiled=True,
    )
    returned = returned.reshape(expert_total * capacity, model_width)
    gathered = returned[slot_ids.reshape(-1)].reshape(own_len, top_count, model_width)
    weights_here = combine_weights.reshape(own_len, top_count)
    mixture = jnp.sum(weights_here[..., None] * gathered.astype(jnp.float32), axis=1)
    layer_out = (residual.astype(jnp.float32) + mixture).astype(jnp.bfloat16)
    return layer_out[None]


def solution(mesh):
    return jax.shard_map(
        body,
        mesh=mesh,
        in_specs=(
            P(None, ("ctx", "pair"), None),
            P(),
            P(None, ("head", "pair")),
            P(("head", "pair"), None),
            P(("head", "pair"), None),
            P(None, ("head", "pair")),
            P(),
            P("head", ("ctx", "pair"), None),
            P("head", ("ctx", "pair"), None),
            P(("ctx", "head"), "pair", None),
            P(("ctx", "head"), "pair", None),
            P(("ctx", "head"), "pair", None),
        ),
        out_specs=P("head", ("ctx", "pair"), None),
        check_vma=False,
    )
```

profile of v0, /device:TPU:0, one launch (start us, length us, event | category | flops | bytes accessed | tf_op | source)
XLA Modules:
  0.0 205.9 jit_solution(12131106147591064016)
XLA Ops:
  6.5 0.7 all-gather.8.cloned.1.call-update
  7.3 0.7 all-gather.10.cloned.1.call-update
  8.1 0.7 all-gather.12.cloned.1.call-update
  8.8 0.1 fusion.31
  8.9 0.1 fusion.33
  9.0 7.1 %all_gather.27 = bf16[2,32,2048]{2,1,0:T(8,128)(2,1)S(1)} all-gather(bf16[2,16,2048]{2,1,0:T(8,128)(2,1)S(1)} %fusion.33), channel_id=1, replica_groups=mesh['ctx'=8,'head'=2,'pair'=2] {'pair'}, dimensions={1}, use_global_device_ids=true | all-gather | bytes 393216 | tf_op jit(solution)/shard_map/all_gather | solution.py:54
  16.1 0.5 fusion.13
  16.7 0.1 fusion.66
  16.8 0.1 multiply_cosine_fusion
  17.1 0.2 convolution_convert_fusion.4
  17.3 0.1 copy.91
  17.5 4.6 %all_gather.28 = bf16[2,32,128]{1,0,2:T(2,128)(2,1)S(1)} all-gather(bf16[2,32,64]{1,0,2:T(2,128)(2,1)S(1)} %copy.91), channel_id=1, replica_groups=mesh['ctx'=8,'head'=2,'pair'=2] {'pair'}, dimensions={2}, use_global_device_ids=true | all-gather | bytes 24576 | tf_op jit(solution)/shard_map/all_gather | solution.py:63
  22.2 0.1 pad_maximum_fusion.1
  22.4 31.2 %all-gather = bf16[2,256,1,128]{3,0,2,1:T(2,128)(2,1)S(1)} all-gather(bf16[2,32,1,128]{3,0,2,1:T(2,128)(2,1)S(1)} %copy.94), channel_id=2, replica_groups=mesh['ctx'=8,'head'=2,'pair'=2] {'ctx'}, dimensions={1}, use_global_device_ids=true | all-gather | bytes 147456 | tf_op jit(solution)/shard_map/all_gather | solution.py:89
  53.6 0.2 convolution_convert_fusion.3
  53.9 4.6 %all_gather.30 = bf16[2,32,128]{1,0,2:T(2,128)(2,1)S(1)} all-gather(bf16[2,32,64]{1,0,2:T(2,128)(2,1)S(1)} %copy.95), channel_id=1, replica_groups=mesh['ctx'=8,'head'=2,'pair'=2] {'pair'}, dimensions={2}, use_global_device_ids=true | all-gather | bytes 24576 | tf_op jit(solution)/shard_map/all_gather | solution.py:66
  58.6 30.6 %all_gather.31 = bf16[2,256,128]{2,0,1:T(2,128)(2,1)S(1)} all-gather(bf16[2,32,128]{2,0,1:T(2,128)(2,1)S(1)} %copy.96), channel_id=1, replica_groups=mesh['ctx'=8,'head'=2,'pair'=2] {'ctx'}, dimensions={1}, use_global_device_ids=true | all-gather | bytes 147456 | tf_op jit(solution)/shard_map/all_gather | solution.py:90
  89.3 0.8 conditional.1
  89.4 0.3 fusion.65
  89.7 0.2 fusion.3
  90.0 0.2 fusion.2
  90.2 0.1 copy_bitcast_fusion
  90.3 13.4 %all_gather.32 = bf16[2,32,2048]{2,1,0:T(8,128)(2,1)S(1)} all-gather(bf16[2,32,512]{2,1,0:T(8,128)(2,1)S(1)} %copy_bitcast_fusion), channel_id=1, replica_groups=mesh['ctx'=8,'head'=2,'pair'=2] {'head','pair'}, dimensions={2}, use_global_device_ids=true | all-gather | bytes 327680 | tf_op jit(solution)/shard_map/all_gather | solution.py:123
  103.7 2.7 %fusion.27 = bf16[2,32,512]{2,1,0:T(8,128)(2,1)} fusion(bf16[2,32,2048]{2,1,0:T(8,128)(2,1)S(1)} %all_gather.32, bf16[2048,512]{1,0:T(8,128)(2,1)} %param.19), kind=kOutput, calls=%fused_computation.42 | convolution fusion | flops 134250496 | bytes 2424832 | tf_op jit(solution)/shard_map/sph,hc->spc/dot_general | solution.py:121
  106.4 3.3 %all-to-all-start = ((bf16[4,16,512]{2,1,0:T(8,128)(2,1)}), bf16[4,16,512]{2,1,0:T(8,128)(2,1)S(1)}, u32[]{:S(2)}, u32[]{:S(2)}) async-start(bf16[4,16,512]{2,1,0:T(8,128)(2,1)} %bitcast.9), calls=%async_computation | async-start | bytes 131072 | tf_op jit(solution)/shard_map/all_to_all | solution.py:130
  110.0 0.2 reduce_window_sum.11
  110.2 0.2 select_reduce_fusion
  110.6 0.1 fusion.53
  110.7 3.1 %all-to-all-done = bf16[4,16,512]{2,1,0:T(8,128)(2,1)S(1)} async-done(((bf16[4,16,512]{2,1,0:T(8,128)(2,1)}), bf16[4,16,512]{2,1,0:T(8,128)(2,1)S(1)}, u32[]{:S(2)}, u32[]{:S(2)}) %all-to-all-start) | async-done | bytes 65568 | tf_op jit(solution)/shard_map/all_to_all | solution.py:130
  114.0 0.1 fusion.49
  114.1 1.2 convolution_convert_fusion.2
  115.3 1.4 reshape.196
  116.7 30.3 %all_to_all.19 = bf16[16,9,2048]{2,1,0:T(8,128)(2,1)} all-to-all(bf16[16,9,2048]{2,1,0:T(8,128)(2,1)S(1)} %reshape.196), channel_id=1, replica_groups=mesh['ctx'=8,'head'=2,'pair'=2] {'ctx','head'}, dimensions={0} | all-to-all | bytes 1179648 | tf_op jit(solution)/shard_map/all_to_all | solution.py:154
  147.0 1.5 reshape.197
  148.6 2.7 %fusion.19 = f32[384,144]{0,1:T(8,128)} fusion(bf16[144,2048]{1,0:T(8,128)(2,1)S(1)} %reshape.197, bf16[1,768,2048]{2,1,0:T(8,128)(2,1)} %all-gather.8.cloned.1.call-done), kind=kOutput, calls=%fused_computation.34 | convolution fusion | flops 226492416 | bytes 2383872 | tf_op jit(solution)/shard_map/dot_general | solution.py:173
  151.3 3.3 %all-gather.12.cloned.1.call-done = bf16[1,768,2048]{2,1,0:T(8,128)(2,1)} async-done(((bf16[1,384,2048]{2,1,0:T(8,128)(2,1)}), bf16[1,768,2048]{2,1,0:T(8,128)(2,1)}) %all-gather.12.cloned.1.call-update) | async-done | bytes 3145744 | tf_op jit(solution)/shard_map/all_gather | solution.py:170
  154.6 3.3 %convolution_convert_fusion.1 = bf16[144,2048]{1,0:T(8,128)(2,1)S(1)} fusion(bf16[1,768,2048]{2,1,0:T(8,128)(2,1)} %all-gather.12.cloned.1.call-done, bf16[144,2048]{1,0:T(8,128)(2,1)S(1)} %reshape.197, bf16[1,768,2048]{2,1,0:T(8,128)(2,1)} %all-gather.10.cloned.1.call-done, f32[384,144]{0,1:T(8,128)} %fusion.19), kind=kOutput, calls=%fused_computation.17 | convolution fusion | flops 453611520 | bytes 4546560 | tf_op jit(solution)/shard_map/dot_general | solution.py:186
  157.9 2.7 %fusion.22 = f32[384,144]{0,1:T(8,128)} fusion(bf16[144,2048]{1,0:T(8,128)(2,1)S(1)} %reshape.197, bf16[1,768,2048]{2,1,0:T(8,128)(2,1)} %all-gather.8.cloned.1.call-done), kind=kOutput, calls=%fused_computation.37 | convolution fusion | flops 226492416 | bytes 2383872 | tf_op jit(solution)/shard_map/dot_general | solution.py:173
  160.6 4.1 %convolution_convert_fusion = bf16[144,2048]{1,0:T(8,128)(2,1)} fusion(bf16[1,768,2048]{2,1,0:T(8,128)(2,1)} %all-gather.12.cloned.1.call-done, bf16[144,2048]{1,0:T(8,128)(2,1)S(1)} %reshape.197, bf16[1,768,2048]{2,1,0:T(8,128)(2,1)} %all-gather.10.cloned.1.call-done, f32[384,144]{0,1:T(8,128)} %fusion.22), kind=kOutput, calls=%fused_computation.16 | convolution fusion | flops 453611520 | bytes 4546560 | tf_op jit(solution)/shard_map/dot_general | solution.py:186
  164.7 1.2 add_convert_fusion
  165.9 1.3 reshape.198
  167.2 5.7 %all-to-all-start.2 = ((bf16[16,9,2048]{2,1,0:T(8,128)(2,1)}), bf16[16,9,2048]{2,1,0:T(8,128)(2,1)}, u32[]{:S(2)}, u32[]{:S(2)}) async-start(bf16[16,9,2048]{2,1,0:T(8,128)(2,1)} %reshape.198), calls=%async_computation.2 | async-start | bytes 2097152 | tf_op jit(solution)/shard_map/all_to_all | solution.py:197
  173.1 0.7 copy.116
  173.8 22.1 %all-to-all-done.2 = bf16[16,9,2048]{2,1,0:T(8,128)(2,1)} async-done(((bf16[16,9,2048]{2,1,0:T(8,128)(2,1)}), bf16[16,9,2048]{2,1,0:T(8,128)(2,1)}, u32[]{:S(2)}, u32[]{:S(2)}) %all-to-all-start.2) | async-done | bytes 589856 | tf_op jit(solution)/shard_map/all_to_all | solution.py:197
  195.8 1.5 reshape.199
  197.3 0.9 gather_fusion
  198.3 0.4 fusion.30
  198.7 0.7 fusion.52
  (57 shorter events, 1.9 us)
Async XLA Ops:
  6.5 9.6 %copy-start = (bf16[2048,512]{1,0:T(8,128)(2,1)S(1)}, bf16[2048,512]{1,0:T(8,128)(2,1)}, u32[]{:S(2)}) copy-start(bf16[2048,512]{1,0:T(8,128)(2,1)} %param.16) | copy-start | bytes 6291460
  6.5 2.2 %copy-start.1 = (bf16[2,16,2048]{2,1,0:T(8,128)(2,1)S(1)}, bf16[2,16,2048]{2,1,0:T(8,128)(2,1)}, u32[]{:S(2)}) copy-start(bf16[2,16,2048]{2,1,0:T(8,128)(2,1)} %param.14) | copy-start | bytes 393220
  6.5 2.4 %copy-start.7 = (f32[2048]{0:T(1024)S(1)}, f32[2048]{0:T(1024)}, u32[]{:S(2)}) copy-start(f32[2048]{0:T(1024)} %param.15) | copy-start | bytes 24580
  6.5 142.0 %all-gather.8.cloned.1.call-start = ((), (), s32[]{:S(2)}) async-start(), calls=%async_computation.3 | async-start | bytes 4718592 | tf_op jit(solution)/shard_map/all_gather | solution.py:168
  7.3 144.0 %all-gather.10.cloned.1.call-start = ((), (), s32[]{:S(2)}) async-start(), calls=%async_computation.4 | async-start | bytes 4718592 | tf_op jit(solution)/shard_map/all_gather | solution.py:169
  8.0 146.6 %all-gather.12.cloned.1.call-start = ((), (), s32[]{:S(2)}) async-start(), calls=%async_computation.5 | async-start | bytes 4718592 | tf_op jit(solution)/shard_map/all_gather | solution.py:170
  8.8 8.3 %copy-start.3 = (bf16[64,2048]{1,0:T(8,128)(2,1)S(1)}, bf16[64,2048]{1,0:T(8,128)(2,1)}, u32[]{:S(2)}) copy-start(bf16[64,2048]{1,0:T(8,128)(2,1)} %param.17) | copy-start | bytes 786436
  16.1 37.5 %copy-start.4 = (bf16[64,2048]{1,0:T(8,128)(2,1)S(1)}, bf16[64,2048]{1,0:T(8,128)(2,1)}, u32[]{:S(2)}) copy-start(bf16[64,2048]{1,0:T(8,128)(2,1)} %param.18) | copy-start | bytes 786436
  89.3 20.4 %copy-start.5 = (s32[1,16,8]{1,2,0:T(8,128)S(1)}, s32[1,16,8]{1,2,0:T(8,128)}, u32[]{:S(2)}) copy-start(s32[1,16,8]{1,2,0:T(8,128)} %param.21) | copy-start | bytes 1540
  103.7 10.4 %copy-start.6 = (f32[2048]{0:T(1024)S(1)}, f32[2048]{0:T(1024)}, u32[]{:S(2)}) copy-start(f32[2048]{0:T(1024)} %param.20) | copy-start | bytes 24580
  106.4 7.4 %all-to-all-start = ((bf16[4,16,512]{2,1,0:T(8,128)(2,1)}), bf16[4,16,512]{2,1,0:T(8,128)(2,1)S(1)}, u32[]{:S(2)}, u32[]{:S(2)}) async-start(bf16[4,16,512]{2,1,0:T(8,128)(2,1)} %bitcast.9), calls=%async_computation | async-start | bytes 131072 | tf_op jit(solution)/shard_map/all_to_all | solution.py:130
  165.9 7.1 %copy-start.8 = (f32[1,16,8]{1,2,0:T(8,128)S(1)}, f32[1,16,8]{1,2,0:T(8,128)}, u32[]{:S(2)}) copy-start(f32[1,16,8]{1,2,0:T(8,128)} %param.22) | copy-start | bytes 1540
  167.2 28.7 %all-to-all-start.2 = ((bf16[16,9,2048]{2,1,0:T(8,128)(2,1)}), bf16[16,9,2048]{2,1,0:T(8,128)(2,1)}, u32[]{:S(2)}, u32[]{:S(2)}) async-start(bf16[16,9,2048]{2,1,0:T(8,128)(2,1)} %reshape.198), calls=%async_computation.2 | async-start | bytes 2097152 | tf_op jit(solution)/shard_map/all_to_all | solution.py:197
  197.3 1.4 copy-start.2
Sparse Core Ops, SparseCore 0:
  8.9 47.9 all-gather.7
  58.5 49.5 all-gather.9
  109.6 44.9 all-gather.11
where the time goes:
time: 208 us; the launch traced here: 206 us
  blocking collectives  122 us (59%)
  waiting for transfers between devices  30.6 us (15%)
  matrix products  18.1 us (9%)
  between operations  13.4 us (6%)
  starting transfers between devices  9.03 us (4%)
  local copies, waits for them, and re-layouts  8.71 us (4%)
  other arithmetic  4.2 us (2%)
    all_gather x1, blocking collectives, body(): key_rows = lax.all_gather(rotated_keys, 'ctx', axis=1, tiled=True)  31.2 us
    all_gather x1, blocking collectives, body(): value_rows = lax.all_gather(every_value_row, 'ctx', axis=1, tiled=True)  30.6 us
    all_to_all x1, blocking collectives, body(): lax.all_to_all(outgoing.reshape(expert_total, capacity, model_width), ('c...  30.3 us
    all_to_all x1, waiting for transfers between devices, body(): lax.all_to_all(expert_out.reshape(expert_total, capacity, model_width), (...  22.1 us
    all_gather x1, blocking collectives, body(): lax.all_gather(attended, ('head', 'pair'), axis=2, tiled=True)  13.4 us
    dot_general x2, matrix products, body(): lax.dot_general(hidden, down_rows_w[lower_row:lower_row + quarter], (((0,...  7.38 us
    all_gather x1, blocking collectives, body(): block_rows = lax.all_gather(normalized_input, 'pair', axis=1, tiled=True)  7.09 us
    all_to_all x1, starting transfers between devices, body(): lax.all_to_all(expert_out.reshape(expert_total, capacity, model_width), (...  5.67 us
  transfers between devices with their start and end apart: 5, of which 3 were waited for; matrix products, arithmetic and copies ran while one was open for 7% of the time, Pallas kernels for 0%

commit v1 on v0

--- a/solution.py
+++ b/solution.py
@@ -1,6 +1,11 @@
+import functools
+
 import jax
 import jax.numpy as jnp
+import numpy as np
 from jax import lax
+from jax.experimental import pallas as pl
+from jax.experimental.pallas import tpu as pltpu
 from jax.sharding import PartitionSpec as P
 
 ROPE_BASE = 1000000.0
@@ -140,8 +145,16 @@
     capacity = max(2, (own_len * top_count + expert_total - 1) // expert_total + 1)
     picked = chosen_experts.reshape(own_len, top_count)
     member = (picked[..., None] == jnp.arange(expert_total)[None, None, :]).astype(jnp.int32)
-    running = jnp.cumsum(member.reshape(own_len * top_count, expert_total), axis=0).reshape(
-        own_len, top_count, expert_total
+    flat_count = own_len * top_count
+    earlier = jnp.tril(jnp.ones((flat_count, flat_count), jnp.bfloat16))
+    running = (
+        jnp.dot(
+            earlier,
+            member.reshape(flat_count, expert_total).astype(jnp.bfloat16),
+            preferred_element_type=jnp.float32,
+        )
+        .astype(jnp.int32)
+        .reshape(own_len, top_count, expert_total)
     )
     slot_rank = jnp.sum((running - 1) * member, axis=-1)
     slot_ids = picked * capacity + slot_rank
@@ -209,9 +222,462 @@
     return layer_out[None]
 
 
+MESH = pl.DeviceIdType.MESH
+PEERS = ("z1", "z2", "z3", "x", "y", "c", "cx")
+LANES = 128
+
+
+def flip(value, bits):
+    if bits & 1:
+        value = value + 1 - 2 * (value % 2)
+    if bits & 2:
+        value = (value + 2) % 4
+    return value
+
+
+def layer_kernel(
+    expert_total,
+    tokens,
+    attn_gain,
+    wq_hbm,
+    wk_hbm,
+    wv_hbm,
+    wo_hbm,
+    moe_gain,
+    chosen,
+    combine,
+    gate_hbm,
+    up_hbm,
+    down_hbm,
+    cos_table,
+    sin_table,
+    out,
+    wq,
+    wk,
+    wv,
+    wo,
+    gate,
+    up,
+    down,
+    rows,
+    kv,
+    attended,
+    projected,
+    owned,
+    gathered,
+    partial,
+    from_core,
+    from_diag,
+    from_x,
+    from_y,
+    from_z,
+    load_sem,
+    send_sem,
+    recv_sem,
+):
+    f32, bf16 = jnp.float32, jnp.bfloat16
+    ctx, h, x = lax.axis_index("ctx"), lax.axis_index("head"), lax.axis_index("pair")
+    z, y = ctx // 2, ctx % 2
+    ox, oy, oh = 1 - x, 1 - y, 1 - h
+    seqs, own, width = tokens.shape
+    block = own * 2
+    head_dim = 2 * wk.shape[0]
+    heads = wq.shape[1] // head_dim
+
+    def peer(name):
+        pz, py, ph, px = z, y, h, x
+        if name[0] == "z":
+            pz = flip(z, int(name[1]))
+        if "c" in name:
+            ph = oh
+        if "x" in name:
+            px = ox
+        if "y" in name:
+            py = oy
+        return {"ctx": pz * 2 + py, "head": ph, "pair": px}
+
+    loads = []
+    for i, (a, b) in enumerate(
+        (
+            (wk_hbm, wk),
+            (wv_hbm, wv),
+            (wq_hbm, wq),
+            (wo_hbm, wo),
+            (gate_hbm.at[0], gate),
+            (up_hbm.at[0], up),
+            (down_hbm.at[0], down),
+        )
+    ):
+        loads.append(pltpu.make_async_copy(a, b, load_sem.at[i]))
+        loads[-1].start()
+
+    barrier = pltpu.get_barrier_semaphore()
+    for name in PEERS:
+        pl.semaphore_signal(barrier, inc=1, device_id=peer(name), device_id_type=MESH)
+
+    number = {}
+    sent = []
+
+    def copy(tag, src, dst, name):
+        i = number.setdefault(tag, len(number))
+        return pltpu.make_async_remote_copy(
+            src_ref=src,
+            dst_ref=dst,
+            send_sem=send_sem.at[i],
+            recv_sem=recv_sem.at[i],
+            device_id=peer(name),
+            device_id_type=MESH,
+        )
+
+    def send(tag, src, dst, name):
+        c = copy(tag, src, dst, name)
+        c.start()
+        sent.append(c)
+
+    def arrive(tag, ref, name):
+        copy(tag, ref, ref, name).wait_recv()
+
+    def norm(values, gain):
+        mean_square = jnp.mean(values * values, axis=-1, keepdims=True)
+        return (values * lax.rsqrt(mean_square + EPSILON) * gain).astype(bf16)
+
+    for s in range(seqs):
+        rows[x, s] = norm(tokens[s].astype(f32), attn_gain[...])
+    pl.semaphore_wait(barrier, len(PEERS))
+    send("rows", rows.at[x], rows.at[x], "x")
+
+    def ordered(j):
+        return jnp.concatenate([rows[0, j], rows[1, j]], axis=0)
+
+    arrive("rows", rows.at[ox], "x")
+    flat = jnp.concatenate([ordered(s) for s in range(seqs)], axis=0)
+    nt = (((1,), (1,)), ((), ()))
+    loads[0].wait()
+    loads[1].wait()
+    both = jnp.concatenate([wk[...], wv[...]], axis=0)
+    kv_part = lax.dot_general(flat, both, nt, preferred_element_type=f32).astype(bf16)
+    for s in range(seqs):
+        kv[x, z, y, s] = kv_part[s * block : (s + 1) * block]
+
+    def plane_start(label, at, first):
+        for k in (3, 2, 1):
+            send(f"{label}z{k}", at(x, z, y), at(x, z, y), f"z{k}")
+        send(f"{label}x0", at(x, z, y), at(x, z, y), "x")
+        send(f"{label}y0", at(x, z, y), at(x, z, y), "y")
+        if first is not None:
+            first("o0", at(x, z, y))
+
+    def plane_rest(label, at, first):
+        for k in (1, 2, 3):
+            zk = flip(z, k)
+            arrive(f"{label}z{k}", at(x, zk, y), f"z{k}")
+            send(f"{label}x{k}", at(x, zk, y), at(x, zk, y), "x")
+            send(f"{label}y{k}", at(x, zk, y), at(x, zk, y), "y")
+            if first is not None:
+                first(f"o{k}", at(x, zk, y))
+        for k in range(4):
+            zk = flip(z, k)
+            arrive(f"{label}x{k}", at(ox, zk, y), "x")
+            if k < 2:
+                send(f"{label}yd{k}", at(ox, zk, y), at(ox, zk, y), "y")
+            if first is not None:
+                first(f"x{k}", at(ox, zk, y))
+            arrive(f"{label}y{k}", at(x, zk, oy), "y")
+            if k >= 2:
+                send(f"{label}xd{k}", at(x, zk, oy), at(x, zk, oy), "x")
+            if first is not None:
+                first(f"y{k}", at(x, zk, oy))
+
+    def plane_diag(label, at, first):
+        for k in range(4):
+            zk = flip(z, k)
+            arrive(f"{label}{'y' if k < 2 else 'x'}d{k}", at(ox, zk, oy), "y" if k < 2 else "x")
+            if first is not None:
+                first(f"d{k}", at(ox, zk, oy))
+
+    def kv_at(px, pz, py):
+        return kv.at[px, pz, py]
+
+    plane_start("kv", kv_at, None)
+
+    loads[2].wait()
+    start = pl.multiple_of(ctx * block, block)
+    cos_here = cos_table[pl.ds(start, block), :]
+    sin_here = sin_table[pl.ds(start, block), :]
+    cos_both = jnp.concatenate([cos_here] * seqs, axis=0)
+    sin_both = jnp.concatenate([sin_here] * seqs, axis=0)
+    half = head_dim // 2
+    queries = []
+    for j in range(heads):
+        q = jnp.dot(flat, wq[:, j * head_dim : (j + 1) * head_dim], preferred_element_type=f32)
+        queries.append((q * cos_both + pltpu.roll(q, half, 1) * sin_both).astype(bf16))
+
+    plane_rest("kv", kv_at, None)
+    plane_diag("kv", kv_at, None)
+
+    span = cos_table.shape[0]
+    lane = lax.broadcasted_iota(jnp.int32, (span, head_dim), 1)
+    row_pos = start + lax.broadcasted_iota(jnp.int32, (heads * block, span), 0) % block
+    allowed = lax.broadcasted_iota(jnp.int32, (heads * block, span), 1) <= row_pos
+    me = h * 2 + x
+    for s in range(seqs):
+        low = kv[0, :, :, s].astype(f32).reshape(span, head_dim)
+        high = kv[1, :, :, s].astype(f32).reshape(span, head_dim)
+        keys = jnp.where(lane < half, low, pltpu.roll(high, half, 1))
+        values = jnp.where(lane < half, pltpu.roll(low, half, 1), high).astype(bf16)
+        keys = (keys * cos_table[...] + pltpu.roll(keys, half, 1) * sin_table[...]).astype(bf16)
+        q = jnp.concatenate([queries[j][s * block : (s + 1) * block] for j in range(heads)], axis=0)
+        scores = lax.dot_general(q, keys, nt, preferred_element_type=f32) * (head_dim**-0.5)
+        scores = jnp.where(allowed, scores, MASKED)
+        weights = jnp.exp(scores - jnp.max(scores, axis=-1, keepdims=True))
+        weights = jnp.where(allowed, weights, 0.0)
+        total = jnp.sum(weights, axis=-1, keepdims=True)
+        mixed = jnp.dot(weights.astype(bf16), values, preferred_element_type=f32) / total
+        mixed = mixed.astype(bf16)
+        for j in range(heads):
+            attended[me, s * block : (s + 1) * block, j * head_dim : (j + 1) * head_dim] = mixed[
+                j * block : (j + 1) * block
+            ]
+    for name in ("cx", "x", "c"):
+        send("at" + name, attended.at[me], attended.at[me], name)
+    group = {"c": (oh, x), "x": (h, ox), "cx": (oh, ox)}
+    part = attended.shape[2]
+
+    loads[3].wait()
+
+    def term(j):
+        at = pl.multiple_of(j * part, part)
+        return jnp.dot(attended[j], wo[pl.ds(at, part), :], preferred_element_type=f32)
+
+    total = term(me)
+    for name in ("c", "x", "cx"):
+        gh, gx = group[name]
+        arrive("at" + name, attended.at[gh * 2 + gx], name)
+        total = total + term(gh * 2 + gx)
+    total = total.astype(bf16)
+    for s in range(seqs):
+        for p in range(2):
+            at = s * block + p * own
+            projected[s, p] = total[at : at + own]
+    for name in ("cx", "x", "c"):
+        gh, gx = group[name]
+        send("pr" + name, projected.at[gh, gx], owned.at[me], name)
+    owned[me] = projected[h, x]
+
+    spot = lax.broadcasted_iota(jnp.int32, (own, LANES), 1)
+    dense = jnp.zeros((own, LANES), f32)
+    for k in range(chosen.shape[2]):
+        w = jnp.broadcast_to(combine[0, :, k : k + 1], (own, LANES))
+        e = jnp.broadcast_to(chosen[0, :, k : k + 1], (own, LANES))
+        top = w.astype(bf16).astype(f32)
+        dense = dense + jnp.where(e == spot, top, 0.0)
+        dense = dense + jnp.where(e + expert_total == spot, w - top, 0.0)
+    gathered[h, y, x, z, :, width:] = dense.astype(bf16)
+
+    for name in ("c", "x", "cx"):
+        gh, gx = group[name]
+        arrive("pr" + name, owned.at[gh * 2 + gx], name)
+    attn_out = jnp.concatenate([owned[j] for j in range(4)], axis=1)
+    residual = (tokens[h].astype(f32) + attn_out.astype(f32)).astype(bf16)
+    gathered[h, y, x, z, :, :width] = norm(residual.astype(f32), moe_gain[...])
+
+    def row_at(px, pz, py):
+        return gathered.at[h, py, px, pz]
+
+    def other_core(tag, ref):
+        send("core" + tag, ref, ref, "c")
+
+    def from_other(tag, px, pz, py):
+        arrive("core" + tag, gathered.at[oh, py, px, pz], "c")
+
+    plane_start("row", row_at, other_core)
+    plane_rest("row", row_at, other_core)
+    for k in range(4):
+        zk = flip(z, k)
+        from_other(f"o{k}", x, zk, y)
+        from_other(f"x{k}", ox, zk, y)
+
+    my_expert = ctx * 2 + h
+    for i in (4, 5, 6):
+        loads[i].wait()
+    per_side = 8 * own
+    tile = min(512, width)
+
+    def run_side(side):
+        tok = jnp.concatenate(
+            [gathered[g, side, :, :, :, :width].reshape(per_side, width) for g in range(2)], axis=0
+        )
+        marks = jnp.concatenate(
+            [gathered[g, side, :, :, :, width:].reshape(per_side, LANES) for g in range(2)], axis=0
+        ).astype(f32)
+        col = lax.broadcasted_iota(jnp.int32, (2 * per_side, LANES), 1)
+        mine = (col == my_expert) | (col == my_expert + expert_total)
+        weight = jnp.sum(jnp.where(mine, marks, 0.0), axis=1, keepdims=True)
+        gate_part = lax.dot_general(tok, gate[...], nt, preferred_element_type=f32)
+        up_part = lax.dot_general(tok, up[...], nt, preferred_element_type=f32)
+        hidden = gate_part / (1.0 + jnp.exp(-gate_part)) * up_part * weight
+        hidden = hidden.astype(bf16)
+        for at in range(0, width, tile):
+            piece = jnp.dot(hidden, down[:, at : at + tile], preferred_element_type=f32).astype(bf16)
+            for g in range(2):
+                partial[g, side, :, :, :, at : at + tile] = piece[
+                    g * per_side : (g + 1) * per_side
+                ].reshape(2, 4, own, tile)
+
+    run_side(y)
+    for q, px in (("x", ox), ("o", x)):
+        send("back" + q, partial.at[oh, y, px], from_core.at[y, px], "c")
+    plane_diag("row", row_at, other_core)
+    for k in range(4):
+        zk = flip(z, k)
+        from_other(f"y{k}", x, zk, oy)
+        from_other(f"d{k}", ox, zk, oy)
+    run_side(oy)
+    for q, px in (("d", ox), ("y", x)):
+        send("back" + q, partial.at[oh, oy, px], from_core.at[oy, px], "c")
+
+    def join(q, py, px):
+        arrive("back" + q, from_core.at[py, px], "c")
+        partial[h, py, px] = (
+            partial[h, py, px].astype(f32) + from_core[py, px].astype(f32)
+        ).astype(bf16)
+
+    join("x", y, ox)
+    join("d", oy, ox)
+    for k in range(4):
+        zk = flip(z, k)
+        send(f"bd{k}", partial.at[h, oy, ox, zk], from_diag.at[k], "x" if k < 2 else "y")
+    for k in (1, 0):
+        send(f"bx{k}", partial.at[h, y, ox, flip(z, k)], from_x.at[k], "x")
+    join("y", oy, x)
+    for k in (3, 2):
+        send(f"by{k}", partial.at[h, oy, x, flip(z, k)], from_y.at[k], "y")
+    join("o", y, x)
+    for k in (3, 2):
+        zk = flip(z, k)
+        arrive(f"bd{k}", from_diag.at[k], "y")
+        partial[h, y, ox, zk] = (
+            partial[h, y, ox, zk].astype(f32) + from_diag[k].astype(f32)
+        ).astype(bf16)
+        send(f"bx{k}", partial.at[h, y, ox, zk], from_x.at[k], "x")
+    for k in (1, 0):
+        zk = flip(z, k)
+        arrive(f"bd{k}", from_diag.at[k], "x")
+        partial[h, oy, x, zk] = (
+            partial[h, oy, x, zk].astype(f32) + from_diag[k].astype(f32)
+        ).astype(bf16)
+        send(f"by{k}", partial.at[h, oy, x, zk], from_y.at[k], "y")
+    result = None
+    for k in (3, 2, 1, 0):
+        zk = flip(z, k)
+        arrive(f"bx{k}", from_x.at[k], "x")
+        arrive(f"by{k}", from_y.at[k], "y")
+        here = partial[h, y, x, zk].astype(f32) + from_x[k].astype(f32) + from_y[k].astype(f32)
+        if k:
+            partial[h, y, x, zk] = here.astype(bf16)
+            send(f"bz{k}", partial.at[h, y, x, zk], from_z.at[k - 1], f"z{k}")
+        else:
+            result = here
+    for k in (1, 2, 3):
+        arrive(f"bz{k}", from_z.at[k - 1], f"z{k}")
+        result = result + from_z[k - 1].astype(f32)
+    out[0] = (residual.astype(f32) + result).astype(bf16)
+    for c in sent:
+        c.wait_send()
+
+
+def fused(*args):
+    (
+        tokens,
+        attn_gain,
+        wq,
+        wk,
+        wv,
+        wo,
+        moe_gain,
+        chosen,
+        combine,
+        gate,
+        up,
+        down,
+    ) = args
+    bf16 = jnp.bfloat16
+    pairs, heads, ctxs = lax.axis_size("pair"), lax.axis_size("head"), lax.axis_size("ctx")
+    seqs, own, width = tokens.shape
+    block = own * pairs
+    span = block * ctxs
+    head_dim = wk.shape[0] * pairs
+    part = wq.shape[1]
+    frequency = ROPE_BASE ** (-2.0 * np.arange(head_dim // 2) / head_dim)
+    angles = np.arange(span)[:, None] * frequency[None, :]
+    cosines, sines = np.cos(angles), np.sin(angles)
+    cos_table = jnp.asarray(np.concatenate([cosines, cosines], axis=1), jnp.float32)
+    sin_table = jnp.asarray(np.concatenate([-sines, sines], axis=1), jnp.float32)
+    vmem = pl.BlockSpec(memory_space=pltpu.VMEM)
+    anywhere = pl.BlockSpec(memory_space=pl.ANY)
+    hidden = gate.shape[1]
+    return pl.pallas_call(
+        functools.partial(layer_kernel, ctxs * heads),
+        out_shape=jax.ShapeDtypeStruct((1, own, width), bf16),
+        in_specs=[vmem, vmem] + [anywhere] * 4 + [vmem] * 3 + [anywhere] * 3 + [vmem] * 2,
+        out_specs=vmem,
+        scratch_shapes=[
+            pltpu.VMEM(wq.shape, bf16),
+            pltpu.VMEM(wk.shape, bf16),
+            pltpu.VMEM(wv.shape, bf16),
+            pltpu.VMEM(wo.shape, bf16),
+            pltpu.VMEM((hidden, width), bf16),
+            pltpu.VMEM((hidden, width), bf16),
+            pltpu.VMEM((hidden, width), bf16),
+            pltpu.VMEM((pairs, seqs, own, width), bf16),
+            pltpu.VMEM((pairs, 4, 2, seqs, block, head_dim), bf16),
+            pltpu.VMEM((4, seqs * block, part), bf16),
+            pltpu.VMEM((seqs, pairs, own, part), bf16),
+            pltpu.VMEM((4, own, part), bf16),
+            pltpu.VMEM((2, 2, 2, 4, own, width + LANES), bf16),
+            pltpu.VMEM((2, 2, 2, 4, own, width), bf16),
+            pltpu.VMEM((2, 2, 4, own, width), bf16),
+            pltpu.VMEM((4, own, width), bf16),
+            pltpu.VMEM((4, own, width), bf16),
+            pltpu.VMEM((4, own, width), bf16),
+            pltpu.VMEM((3, own, width), bf16),
+            pltpu.SemaphoreType.DMA((7,)),
+            pltpu.SemaphoreType.DMA((80,)),
+            pltpu.SemaphoreType.DMA((80,)),
+        ],
+        compiler_params=pltpu.CompilerParams(
+            collective_id=0, has_side_effects=True, vmem_limit_bytes=48 * 2**20
+        ),
+    )(
+        tokens,
+        attn_gain[None],
+        wq,
+        wk,
+        wv,
+        wo,
+        moe_gain[None],
+        chosen,
+        combine,
+        gate,
+        up,
+        down,
+        cos_table,
+        sin_table,
+    )
+
+
+def choose(*args):
+    pairs, heads, ctxs = lax.axis_size("pair"), lax.axis_size("head"), lax.axis_size("ctx")
+    seqs, own, width = args[0].shape
+    experts = ctxs * heads
+    fits = pairs == 2 and heads == 2 and ctxs == 8 and seqs == heads
+    fits = fits and 2 * experts <= LANES and args[3].shape[0] * pairs == LANES
+    return fused(*args) if fits else body(*args)
+
+
 def solution(mesh):
     return jax.shard_map(
-        body,
+        choose,
         mesh=mesh,
         in_specs=(
             P(None, ("ctx", "pair"), None),

time: 208 us -> 80.3 us (0.39)
  blocking collectives: 122 us -> 0 us
  Pallas kernels: 0 us -> 67.5 us
  waiting for transfers between devices: 30.6 us -> 0 us
  matrix products: 18.1 us -> 0 us
  between operations: 13.4 us -> 0.02 us
  starting transfers between devices: 9.03 us -> 0 us
  other arithmetic: 4.2 us -> 0 us
  local copies, waits for them, and re-layouts: 8.71 us -> 12.4 us
    all_gather x6 -> x0, blocking collectives: 91.5 us -> none  [the longest x1 31.2 us: body(): key_rows = lax.all_gather(rotated_keys, 'ctx', axis=1, tiled=True)]
    pallas_call x0 -> x1, Pallas kernels: none -> 67.5 us  [fused(): pl.pallas_call(functools.partial(layer_kernel, ctxs * heads), out_shape=j...]
    all_to_all x1 -> x0, blocking collectives: 30.3 us -> none  [body(): lax.all_to_all(outgoing.reshape(expert_total, capacity, model_width), ('c...]
    all_to_all x2 -> x0, waiting for transfers between devices: 25.1 us -> none  [the longest x1 22.1 us: body(): lax.all_to_all(expert_out.reshape(expert_total, capacity, model_width), (...]
    dot_general x11 -> x0, matrix products: 18.1 us -> none  [the longest x2 7.38 us: body(): lax.dot_general(hidden, down_rows_w[lower_row:lower_row + quarter], (((0,...]
    unnamed x20 -> x23, local copies, waits for them, and re-layouts: 0.16 us -> 12.4 us
    all_to_all x2 -> x0, starting transfers between devices: 8.96 us -> none  [the longest x1 5.67 us: body(): lax.all_to_all(expert_out.reshape(expert_total, capacity, model_width), (...]
    reshape x5 -> x0, local copies, waits for them, and re-layouts: 5.64 us -> none  [the longest x1 1.48 us: body(): incoming = incoming.reshape(expert_total * capacity, model_width)]
  transfers between devices with their start and end apart: 5 -> 0, of which waited for: 3 -> 0; matrix products, arithmetic and copies ran while one was open for 7% -> 0% of each run, Pallas kernels for 0% -> 0%
where the time goes in v1:
time: 80.3 us; the launch traced here: 79.9 us
  Pallas kernels  67.5 us (84%)
  local copies, waits for them, and re-layouts  12.4 us (15%)
    pallas_call x1, Pallas kernels, fused(): pl.pallas_call(functools.partial(layer_kernel, ctxs * heads), out_shape=j...  67.5 us
    unnamed x23, local copies, waits for them, and re-layouts  12.4 us

profile of v1, /device:TPU:0, one launch (start us, length us, event | category | flops | bytes accessed | tf_op | source)
XLA Modules:
  0.0 79.9 jit_solution(2056562821239477194)
XLA Ops:
  0.0 0.8 copy.15.chosen
  0.8 0.8 copy.16.combine
  1.5 0.0 copy-start
  1.5 1.4 %copy-done = bf16[1,384,2048]{2,1,0:T(8,128)(2,1)S(1)} copy-done((bf16[1,384,2048]{2,1,0:T(8,128)(2,1)S(1)}, bf16[1,384,2048]{2,1,0:T(8,128)(2,1)}, u32[]{:S(2)}) %copy-start) | copy-done | bytes 1572888
  2.9 0.0 copy-start.1
  2.9 1.4 %copy-done.1 = bf16[1,384,2048]{2,1,0:T(8,128)(2,1)S(1)} copy-done((bf16[1,384,2048]{2,1,0:T(8,128)(2,1)S(1)}, bf16[1,384,2048]{2,1,0:T(8,128)(2,1)}, u32[]{:S(2)}) %copy-start.1) | copy-done | bytes 1572888
  4.3 0.0 copy-start.2
  4.3 1.4 %copy-done.2 = bf16[1,384,2048]{2,1,0:T(8,128)(2,1)S(1)} copy-done((bf16[1,384,2048]{2,1,0:T(8,128)(2,1)S(1)}, bf16[1,384,2048]{2,1,0:T(8,128)(2,1)}, u32[]{:S(2)}) %copy-start.2) | copy-done | bytes 1572888
  5.7 0.0 copy-start.3
  5.7 0.9 %copy-done.3 = bf16[64,2048]{1,0:T(8,128)(2,1)S(1)} copy-done((bf16[64,2048]{1,0:T(8,128)(2,1)S(1)}, bf16[64,2048]{1,0:T(8,128)(2,1)}, u32[]{:S(2)}) %copy-start.3) | copy-done | bytes 262168
  6.7 0.0 copy-start.4
  6.7 0.9 %copy-done.4 = bf16[64,2048]{1,0:T(8,128)(2,1)S(1)} copy-done((bf16[64,2048]{1,0:T(8,128)(2,1)S(1)}, bf16[64,2048]{1,0:T(8,128)(2,1)}, u32[]{:S(2)}) %copy-start.4) | copy-done | bytes 262168
  7.6 0.0 copy-start.5
  7.6 0.9 %copy-done.5 = bf16[2,16,2048]{2,1,0:T(8,128)(2,1)S(1)} copy-done((bf16[2,16,2048]{2,1,0:T(8,128)(2,1)S(1)}, bf16[2,16,2048]{2,1,0:T(8,128)(2,1)}, u32[]{:S(2)}) %copy-start.5) | copy-done | bytes 131096
  8.5 0.0 copy-start.6
  8.5 0.9 %copy-done.6 = f32[256,128]{1,0:T(8,128)S(1)} copy-done((f32[256,128]{1,0:T(8,128)S(1)}, f32[256,128]{1,0:T(8,128)}, u32[]{:S(2)}) %copy-start.6) | copy-done | bytes 131096
  9.5 0.0 copy-start.7
  9.5 0.9 %copy-done.7 = f32[256,128]{1,0:T(8,128)S(1)} copy-done((f32[256,128]{1,0:T(8,128)S(1)}, f32[256,128]{1,0:T(8,128)}, u32[]{:S(2)}) %copy-start.7) | copy-done | bytes 131096
  10.4 0.0 copy-start.8
  10.4 0.7 copy-done.8
  11.1 0.0 copy-start.9
  11.1 0.7 copy-done.9
  11.8 67.5 %shard_map.136 = bf16[1,16,2048]{2,1,0:T(8,128)(2,1)S(1)} custom-call(bf16[2,16,2048]{2,1,0:T(8,128)(2,1)S(1)} %copy-done.5, f32[1,2048]{1,0:T(1,128)S(1)} %bitcast.2, bf16[2048,512]{1,0:T(8,128)(2,1)} %wq_hbm.1, bf16[64,2048]{1,0:T(8,128)(2,1)S(1)} %copy-done.3, bf16[64,2048]{1,0:T(8,128)(2,1)S(1)} %copy-done.4, bf16[2048,512]{1,0:T(8,128)(2,1)} %wo_hbm.1, ...), custom_call_target="tpu_custom_call" | custom-call | tf_op jit(solution)/shard_map/pallas_call | solution.py:619
  79.2 0.6 copy.18
Async XLA Ops:
  1.5 1.4 %copy-start = (bf16[1,384,2048]{2,1,0:T(8,128)(2,1)S(1)}, bf16[1,384,2048]{2,1,0:T(8,128)(2,1)}, u32[]{:S(2)}) copy-start(bf16[1,384,2048]{2,1,0:T(8,128)(2,1)} %gate_hbm.1) | copy-start | bytes 4718596
  2.9 1.4 %copy-start.1 = (bf16[1,384,2048]{2,1,0:T(8,128)(2,1)S(1)}, bf16[1,384,2048]{2,1,0:T(8,128)(2,1)}, u32[]{:S(2)}) copy-start(bf16[1,384,2048]{2,1,0:T(8,128)(2,1)} %up_hbm.1) | copy-start | bytes 4718596
  4.3 1.4 %copy-start.2 = (bf16[1,384,2048]{2,1,0:T(8,128)(2,1)S(1)}, bf16[1,384,2048]{2,1,0:T(8,128)(2,1)}, u32[]{:S(2)}) copy-start(bf16[1,384,2048]{2,1,0:T(8,128)(2,1)} %down_hbm.1) | copy-start | bytes 4718596
  5.7 0.9 %copy-start.3 = (bf16[64,2048]{1,0:T(8,128)(2,1)S(1)}, bf16[64,2048]{1,0:T(8,128)(2,1)}, u32[]{:S(2)}) copy-start(bf16[64,2048]{1,0:T(8,128)(2,1)} %wk_hbm.1) | copy-start | bytes 786436
  6.7 0.9 %copy-start.4 = (bf16[64,2048]{1,0:T(8,128)(2,1)S(1)}, bf16[64,2048]{1,0:T(8,128)(2,1)}, u32[]{:S(2)}) copy-start(bf16[64,2048]{1,0:T(8,128)(2,1)} %wv_hbm.1) | copy-start | bytes 786436
  7.6 0.9 %copy-start.5 = (bf16[2,16,2048]{2,1,0:T(8,128)(2,1)S(1)}, bf16[2,16,2048]{2,1,0:T(8,128)(2,1)}, u32[]{:S(2)}) copy-start(bf16[2,16,2048]{2,1,0:T(8,128)(2,1)} %tokens.1) | copy-start | bytes 393220
  8.5 0.9 %copy-start.6 = (f32[256,128]{1,0:T(8,128)S(1)}, f32[256,128]{1,0:T(8,128)}, u32[]{:S(2)}) copy-start(f32[256,128]{1,0:T(8,128)} %constant.5.clone.sin_table) | copy-start | bytes 393220
  9.5 0.9 %copy-start.7 = (f32[256,128]{1,0:T(8,128)S(1)}, f32[256,128]{1,0:T(8,128)}, u32[]{:S(2)}) copy-start(f32[256,128]{1,0:T(8,128)} %constant.4.clone.cos_table) | copy-start | bytes 393220
  10.4 0.7 copy-start.8
  11.1 0.7 copy-start.9

commit v2 on v1

--- a/solution.py
+++ b/solution.py
@@ -223,7 +223,7 @@
 
 
 MESH = pl.DeviceIdType.MESH
-PEERS = ("z1", "z2", "z3", "x", "y", "c", "cx")
+PEERS = ("z1", "z2", "z3", "x", "y", "xy", "c", "cx")
 LANES = 128
 
 
@@ -237,21 +237,28 @@
 
 def layer_kernel(
     expert_total,
-    tokens,
-    attn_gain,
+    tokens_hbm,
+    attn_gain_hbm,
     wq_hbm,
     wk_hbm,
     wv_hbm,
     wo_hbm,
+    moe_gain_hbm,
+    chosen_hbm,
+    combine_hbm,
+    gate_hbm,
+    up_hbm,
+    down_hbm,
+    cos_hbm,
+    sin_hbm,
+    out,
+    tokens,
+    attn_gain,
     moe_gain,
     chosen,
     combine,
-    gate_hbm,
-    up_hbm,
-    down_hbm,
     cos_table,
     sin_table,
-    out,
     wq,
     wk,
     wv,
@@ -299,10 +306,17 @@
     loads = []
     for i, (a, b) in enumerate(
         (
+            (tokens_hbm, tokens),
+            (attn_gain_hbm, attn_gain),
             (wk_hbm, wk),
             (wv_hbm, wv),
             (wq_hbm, wq),
+            (cos_hbm, cos_table),
+            (sin_hbm, sin_table),
             (wo_hbm, wo),
+            (moe_gain_hbm, moe_gain),
+            (chosen_hbm.at[0], chosen),
+            (combine_hbm.at[0], combine),
             (gate_hbm.at[0], gate),
             (up_hbm.at[0], up),
             (down_hbm.at[0], down),
@@ -341,6 +355,8 @@
         mean_square = jnp.mean(values * values, axis=-1, keepdims=True)
         return (values * lax.rsqrt(mean_square + EPSILON) * gain).astype(bf16)
 
+    loads[0].wait()
+    loads[1].wait()
     for s in range(seqs):
         rows[x, s] = norm(tokens[s].astype(f32), attn_gain[...])
     pl.semaphore_wait(barrier, len(PEERS))
@@ -352,25 +368,29 @@
     arrive("rows", rows.at[ox], "x")
     flat = jnp.concatenate([ordered(s) for s in range(seqs)], axis=0)
     nt = (((1,), (1,)), ((), ()))
-    loads[0].wait()
-    loads[1].wait()
+    loads[2].wait()
+    loads[3].wait()
     both = jnp.concatenate([wk[...], wv[...]], axis=0)
     kv_part = lax.dot_general(flat, both, nt, preferred_element_type=f32).astype(bf16)
     for s in range(seqs):
         kv[x, z, y, s] = kv_part[s * block : (s + 1) * block]
 
-    def plane_start(label, at, first):
+    def plane_start(label, at, first, direct):
         for k in (3, 2, 1):
             send(f"{label}z{k}", at(x, z, y), at(x, z, y), f"z{k}")
         send(f"{label}x0", at(x, z, y), at(x, z, y), "x")
         send(f"{label}y0", at(x, z, y), at(x, z, y), "y")
+        if direct:
+            send(f"{label}d0", at(x, z, y), at(x, z, y), "xy")
         if first is not None:
             first("o0", at(x, z, y))
 
-    def plane_rest(label, at, first):
+    def plane_rest(label, at, first, direct):
         for k in (1, 2, 3):
             zk = flip(z, k)
             arrive(f"{label}z{k}", at(x, zk, y), f"z{k}")
+            if direct:
+                send(f"{label}d{k}", at(x, zk, y), at(x, zk, y), "xy")
             send(f"{label}x{k}", at(x, zk, y), at(x, zk, y), "x")
             send(f"{label}y{k}", at(x, zk, y), at(x, zk, y), "y")
             if first is not None:
@@ -378,29 +398,34 @@
         for k in range(4):
             zk = flip(z, k)
             arrive(f"{label}x{k}", at(ox, zk, y), "x")
-            if k < 2:
+            if k < 2 and not direct:
                 send(f"{label}yd{k}", at(ox, zk, y), at(ox, zk, y), "y")
             if first is not None:
                 first(f"x{k}", at(ox, zk, y))
             arrive(f"{label}y{k}", at(x, zk, oy), "y")
-            if k >= 2:
+            if k >= 2 and not direct:
                 send(f"{label}xd{k}", at(x, zk, oy), at(x, zk, oy), "x")
             if first is not None:
                 first(f"y{k}", at(x, zk, oy))
 
-    def plane_diag(label, at, first):
+    def plane_diag(label, at, first, direct):
         for k in range(4):
             zk = flip(z, k)
-            arrive(f"{label}{'y' if k < 2 else 'x'}d{k}", at(ox, zk, oy), "y" if k < 2 else "x")
+            if direct:
+                arrive(f"{label}d{k}", at(ox, zk, oy), "xy")
+            else:
+                way = "y" if k < 2 else "x"
+                arrive(f"{label}{way}d{k}", at(ox, zk, oy), way)
             if first is not None:
                 first(f"d{k}", at(ox, zk, oy))
 
     def kv_at(px, pz, py):
         return kv.at[px, pz, py]
 
-    plane_start("kv", kv_at, None)
-
-    loads[2].wait()
+    plane_start("kv", kv_at, None, True)
+
+    for i in (4, 5, 6):
+        loads[i].wait()
     start = pl.multiple_of(ctx * block, block)
     cos_here = cos_table[pl.ds(start, block), :]
     sin_here = sin_table[pl.ds(start, block), :]
@@ -412,8 +437,8 @@
         q = jnp.dot(flat, wq[:, j * head_dim : (j + 1) * head_dim], preferred_element_type=f32)
         queries.append((q * cos_both + pltpu.roll(q, half, 1) * sin_both).astype(bf16))
 
-    plane_rest("kv", kv_at, None)
-    plane_diag("kv", kv_at, None)
+    plane_rest("kv", kv_at, None, True)
+    plane_diag("kv", kv_at, None, True)
 
     span = cos_table.shape[0]
     lane = lax.broadcasted_iota(jnp.int32, (span, head_dim), 1)
@@ -438,12 +463,13 @@
             attended[me, s * block : (s + 1) * block, j * head_dim : (j + 1) * head_dim] = mixed[
                 j * block : (j + 1) * block
             ]
-    for name in ("cx", "x", "c"):
-        send("at" + name, attended.at[me], attended.at[me], name)
+        for name in ("cx", "x", "c"):
+            ref = attended.at[me, pl.ds(s * block, block)]
+            send(f"at{s}{name}", ref, ref, name)
     group = {"c": (oh, x), "x": (h, ox), "cx": (oh, ox)}
     part = attended.shape[2]
 
-    loads[3].wait()
+    loads[7].wait()
 
     def term(j):
         at = pl.multiple_of(j * part, part)
@@ -452,7 +478,8 @@
     total = term(me)
     for name in ("c", "x", "cx"):
         gh, gx = group[name]
-        arrive("at" + name, attended.at[gh * 2 + gx], name)
+        for s in range(seqs):
+            arrive(f"at{s}{name}", attended.at[gh * 2 + gx, pl.ds(s * block, block)], name)
         total = total + term(gh * 2 + gx)
     total = total.astype(bf16)
     for s in range(seqs):
@@ -464,14 +491,22 @@
         send("pr" + name, projected.at[gh, gx], owned.at[me], name)
     owned[me] = projected[h, x]
 
-    spot = lax.broadcasted_iota(jnp.int32, (own, LANES), 1)
-    dense = jnp.zeros((own, LANES), f32)
-    for k in range(chosen.shape[2]):
-        w = jnp.broadcast_to(combine[0, :, k : k + 1], (own, LANES))
-        e = jnp.broadcast_to(chosen[0, :, k : k + 1], (own, LANES))
+    for i in (8, 9, 10):
+        loads[i].wait()
+    spot = lax.broadcasted_iota(jnp.int32, (LANES, own), 0)
+    dense = jnp.zeros((LANES, own), f32)
+    for k in range(chosen.shape[0]):
+        w = jnp.broadcast_to(combine[k : k + 1, :], (LANES, own))
+        e = jnp.broadcast_to(chosen[k : k + 1, :], (LANES, own))
         top = w.astype(bf16).astype(f32)
         dense = dense + jnp.where(e == spot, top, 0.0)
         dense = dense + jnp.where(e + expert_total == spot, w - top, 0.0)
+    ones = lax.broadcasted_iota(jnp.int32, (own, own), 0) == lax.broadcasted_iota(
+        jnp.int32, (own, own), 1
+    )
+    dense = lax.dot_general(
+        jnp.where(ones, 1.0, 0.0).astype(bf16), dense.astype(bf16), nt, preferred_element_type=f32
+    )
     gathered[h, y, x, z, :, width:] = dense.astype(bf16)
 
     for name in ("c", "x", "cx"):
@@ -490,15 +525,15 @@
     def from_other(tag, px, pz, py):
         arrive("core" + tag, gathered.at[oh, py, px, pz], "c")
 
-    plane_start("row", row_at, other_core)
-    plane_rest("row", row_at, other_core)
+    plane_start("row", row_at, other_core, False)
+    plane_rest("row", row_at, other_core, False)
     for k in range(4):
         zk = flip(z, k)
         from_other(f"o{k}", x, zk, y)
         from_other(f"x{k}", ox, zk, y)
 
     my_expert = ctx * 2 + h
-    for i in (4, 5, 6):
+    for i in (11, 12, 13):
         loads[i].wait()
     per_side = 8 * own
     tile = min(512, width)
@@ -527,7 +562,7 @@
     run_side(y)
     for q, px in (("x", ox), ("o", x)):
         send("back" + q, partial.at[oh, y, px], from_core.at[y, px], "c")
-    plane_diag("row", row_at, other_core)
+    plane_diag("row", row_at, other_core, False)
     for k in range(4):
         zk = flip(z, k)
         from_other(f"y{k}", x, zk, oy)
@@ -614,14 +649,21 @@
     cos_table = jnp.asarray(np.concatenate([cosines, cosines], axis=1), jnp.float32)
     sin_table = jnp.asarray(np.concatenate([-sines, sines], axis=1), jnp.float32)
     vmem = pl.BlockSpec(memory_space=pltpu.VMEM)
-    anywhere = pl.BlockSpec(memory_space=pl.ANY)
+    anywhere = pl.BlockSpec(memory_space=pltpu.HBM)
     hidden = gate.shape[1]
     return pl.pallas_call(
         functools.partial(layer_kernel, ctxs * heads),
         out_shape=jax.ShapeDtypeStruct((1, own, width), bf16),
-        in_specs=[vmem, vmem] + [anywhere] * 4 + [vmem] * 3 + [anywhere] * 3 + [vmem] * 2,
+        in_specs=[anywhere] * 14,
         out_specs=vmem,
         scratch_shapes=[
+            pltpu.VMEM(tokens.shape, bf16),
+            pltpu.VMEM((1, width), jnp.float32),
+            pltpu.VMEM((1, width), jnp.float32),
+            pltpu.VMEM((chosen.shape[2], own), chosen.dtype),
+            pltpu.VMEM((chosen.shape[2], own), jnp.float32),
+            pltpu.VMEM((span, head_dim), jnp.float32),
+            pltpu.VMEM((span, head_dim), jnp.float32),
             pltpu.VMEM(wq.shape, bf16),
             pltpu.VMEM(wk.shape, bf16),
             pltpu.VMEM(wv.shape, bf16),
@@ -641,12 +683,12 @@
             pltpu.VMEM((4, own, width), bf16),
             pltpu.VMEM((4, own, width), bf16),
             pltpu.VMEM((3, own, width), bf16),
-            pltpu.SemaphoreType.DMA((7,)),
+            pltpu.SemaphoreType.DMA((14,)),
             pltpu.SemaphoreType.DMA((80,)),
             pltpu.SemaphoreType.DMA((80,)),
         ],
         compiler_params=pltpu.CompilerParams(
-            collective_id=0, has_side_effects=True, vmem_limit_bytes=48 * 2**20
+            collective_id=0, has_side_effects=True, vmem_limit_bytes=60 * 2**20
         ),
     )(
         tokens,
@@ -656,8 +698,8 @@
         wv,
         wo,
         moe_gain[None],
-        chosen,
-        combine,
+        jnp.swapaxes(chosen, 1, 2),
+        jnp.swapaxes(combine, 1, 2),
         gate,
         up,
         down,

time: 80.3 us -> 65.9 us (0.82)
  local copies, waits for them, and re-layouts: 12.4 us -> 1.47 us
  Pallas kernels: 67.5 us -> 64.3 us
    unnamed x23 -> x1, local copies, waits for them, and re-layouts: 12.4 us -> 1.47 us
    pallas_call x1, Pallas kernels: 67.5 us -> 64.3 us  [fused(): pl.pallas_call(functools.partial(layer_kernel, ctxs * heads), out_shape=j...]
where the time goes in v2:
time: 65.9 us; the launch traced here: 65.8 us
  Pallas kernels  64.3 us (98%)
  local copies, waits for them, and re-layouts  1.47 us (2%)
    pallas_call x1, Pallas kernels, fused(): pl.pallas_call(functools.partial(layer_kernel, ctxs * heads), out_shape=j...  64.3 us
    unnamed x1, local copies, waits for them, and re-layouts  1.47 us

profile of v2, /device:TPU:0, one launch (start us, length us, event | category | flops | bytes accessed | tf_op | source)
XLA Modules:
  0.0 65.8 jit_solution(4594531563746263913)
XLA Ops:
  0.0 64.3 %shard_map.136 = bf16[1,16,2048]{2,1,0:T(8,128)(2,1)} custom-call(bf16[2,16,2048]{2,1,0:T(8,128)(2,1)} %tokens_hbm.1, f32[1,2048]{1,0:T(1,128)} %bitcast.4, bf16[2048,512]{1,0:T(8,128)(2,1)} %wq_hbm.1, bf16[64,2048]{1,0:T(8,128)(2,1)} %wk_hbm.1, bf16[64,2048]{1,0:T(8,128)(2,1)} %wv_hbm.1, bf16[2048,512]{1,0:T(8,128)(2,1)} %wo_hbm.1, f32[1,2048]{1,0:T(1,128)} %bitcast.5, ...), custom_call_target="tpu_custom_call" | custom-call | tf_op jit(solution)/shard_map/pallas_call | solution.py:654
  64.3 1.5 %copy.16 = bf16[1,16,2048]{2,1,0:T(8,128)(2,1)} copy(bf16[1,16,2048]{2,1,0:T(8,128)(2,1)} %shard_map.136) | data formatting | bytes 131072

commit v3 on v2

--- a/solution.py
+++ b/solution.py
@@ -376,48 +376,55 @@
         kv[x, z, y, s] = kv_part[s * block : (s + 1) * block]
 
     def plane_start(label, at, first, direct):
-        for k in (3, 2, 1):
-            send(f"{label}z{k}", at(x, z, y), at(x, z, y), f"z{k}")
-        send(f"{label}x0", at(x, z, y), at(x, z, y), "x")
-        send(f"{label}y0", at(x, z, y), at(x, z, y), "y")
+        mine = at(x, z, y)
+        send(f"{label}z1", mine, mine, "z1")
+        send(f"{label}x0", mine, mine, "x")
+        send(f"{label}y0", mine, mine, "y")
+        send(f"{label}z2", mine, mine, "z2")
+        send(f"{label}z3", mine, mine, "z3")
         if direct:
-            send(f"{label}d0", at(x, z, y), at(x, z, y), "xy")
+            send(f"{label}d0", mine, mine, "xy")
         if first is not None:
-            first("o0", at(x, z, y))
+            first("o0", mine)
 
     def plane_rest(label, at, first, direct):
-        for k in (1, 2, 3):
-            zk = flip(z, k)
-            arrive(f"{label}z{k}", at(x, zk, y), f"z{k}")
+        def from_z(k):
+            ref = at(x, flip(z, k), y)
+            arrive(f"{label}z{k}", ref, f"z{k}")
             if direct:
-                send(f"{label}d{k}", at(x, zk, y), at(x, zk, y), "xy")
-            send(f"{label}x{k}", at(x, zk, y), at(x, zk, y), "x")
-            send(f"{label}y{k}", at(x, zk, y), at(x, zk, y), "y")
+                send(f"{label}d{k}", ref, ref, "xy")
+            send(f"{label}x{k}", ref, ref, "x")
+            send(f"{label}y{k}", ref, ref, "y")
             if first is not None:
-                first(f"o{k}", at(x, zk, y))
-        for k in range(4):
-            zk = flip(z, k)
-            arrive(f"{label}x{k}", at(ox, zk, y), "x")
-            if k < 2 and not direct:
-                send(f"{label}yd{k}", at(ox, zk, y), at(ox, zk, y), "y")
+                first(f"o{k}", ref)
+
+        def from_side(way, k):
+            ref = at(ox, flip(z, k), y) if way == "x" else at(x, flip(z, k), oy)
+            arrive(f"{label}{way}{k}", ref, way)
+            on = "y" if k % 2 == 0 else "x"
+            if on != way and not direct:
+                send(f"{label}d{k}", ref, ref, on)
             if first is not None:
-                first(f"x{k}", at(ox, zk, y))
-            arrive(f"{label}y{k}", at(x, zk, oy), "y")
-            if k >= 2 and not direct:
-                send(f"{label}xd{k}", at(x, zk, oy), at(x, zk, oy), "x")
-            if first is not None:
-                first(f"y{k}", at(x, zk, oy))
+                first(f"{way}{k}", ref)
+
+        from_z(1)
+        from_side("x", 0)
+        from_side("y", 0)
+        from_z(2)
+        from_side("y", 1)
+        from_side("x", 1)
+        from_z(3)
+        from_side("x", 2)
+        from_side("y", 2)
+        from_side("y", 3)
+        from_side("x", 3)
 
     def plane_diag(label, at, first, direct):
         for k in range(4):
-            zk = flip(z, k)
-            if direct:
-                arrive(f"{label}d{k}", at(ox, zk, oy), "xy")
-            else:
-                way = "y" if k < 2 else "x"
-                arrive(f"{label}{way}d{k}", at(ox, zk, oy), way)
+            ref = at(ox, flip(z, k), oy)
+            arrive(f"{label}d{k}", ref, "xy" if direct else "y" if k % 2 == 0 else "x")
             if first is not None:
-                first(f"d{k}", at(ox, zk, oy))
+                first(f"d{k}", ref)
 
     def kv_at(px, pz, py):
         return kv.at[px, pz, py]
@@ -577,31 +584,36 @@
             partial[h, py, px].astype(f32) + from_core[py, px].astype(f32)
         ).astype(bf16)
 
+    def diag_send(k):
+        send(f"bd{k}", partial.at[h, oy, ox, flip(z, k)], from_diag.at[k], "x" if k % 2 else "y")
+
+    def side_send(way, k, after_diag):
+        py, px = (y, ox) if way == "x" else (oy, x)
+        zk = flip(z, k)
+        if after_diag:
+            arrive(f"bd{k}", from_diag.at[k], "x" if k % 2 else "y")
+            partial[h, py, px, zk] = (
+                partial[h, py, px, zk].astype(f32) + from_diag[k].astype(f32)
+            ).astype(bf16)
+        there = from_x if way == "x" else from_y
+        send(f"b{way}{k}", partial.at[h, py, px, zk], there.at[k], way)
+
+    join("d", oy, ox)
+    diag_send(3)
+    diag_send(2)
     join("x", y, ox)
-    join("d", oy, ox)
-    for k in range(4):
-        zk = flip(z, k)
-        send(f"bd{k}", partial.at[h, oy, ox, zk], from_diag.at[k], "x" if k < 2 else "y")
-    for k in (1, 0):
-        send(f"bx{k}", partial.at[h, y, ox, flip(z, k)], from_x.at[k], "x")
+    side_send("x", 3, False)
     join("y", oy, x)
-    for k in (3, 2):
-        send(f"by{k}", partial.at[h, oy, x, flip(z, k)], from_y.at[k], "y")
+    side_send("y", 2, False)
+    side_send("y", 3, True)
+    side_send("x", 2, True)
+    diag_send(1)
+    diag_send(0)
+    side_send("x", 1, False)
     join("o", y, x)
-    for k in (3, 2):
-        zk = flip(z, k)
-        arrive(f"bd{k}", from_diag.at[k], "y")
-        partial[h, y, ox, zk] = (
-            partial[h, y, ox, zk].astype(f32) + from_diag[k].astype(f32)
-        ).astype(bf16)
-        send(f"bx{k}", partial.at[h, y, ox, zk], from_x.at[k], "x")
-    for k in (1, 0):
-        zk = flip(z, k)
-        arrive(f"bd{k}", from_diag.at[k], "x")
-        partial[h, oy, x, zk] = (
-            partial[h, oy, x, zk].astype(f32) + from_diag[k].astype(f32)
-        ).astype(bf16)
-        send(f"by{k}", partial.at[h, oy, x, zk], from_y.at[k], "y")
+    side_send("y", 1, True)
+    side_send("y", 0, False)
+    side_send("x", 0, True)
     result = None
     for k in (3, 2, 1, 0):
         zk = flip(z, k)

time: 65.9 us -> 67.2 us (1.020)
  Pallas kernels: 64.3 us -> 65.5 us
    pallas_call x1, Pallas kernels: 64.3 us -> 65.5 us  [fused(): pl.pallas_call(functools.partial(layer_kernel, ctxs * heads), out_shape=j...]
where the time goes in v3:
time: 67.2 us; the launch traced here: 67 us
  Pallas kernels  65.5 us (97%)
  local copies, waits for them, and re-layouts  1.47 us (2%)
    pallas_call x1, Pallas kernels, fused(): pl.pallas_call(functools.partial(layer_kernel, ctxs * heads), out_shape=j...  65.5 us
    unnamed x1, local copies, waits for them, and re-layouts  1.47 us

profile of v3, /device:TPU:0, one launch (start us, length us, event | category | flops | bytes accessed | tf_op | source)
XLA Modules:
  0.0 67.0 jit_solution(12007644380949179180)
XLA Ops:
  0.0 65.5 %shard_map.136 = bf16[1,16,2048]{2,1,0:T(8,128)(2,1)} custom-call(bf16[2,16,2048]{2,1,0:T(8,128)(2,1)} %tokens_hbm.1, f32[1,2048]{1,0:T(1,128)} %bitcast.4, bf16[2048,512]{1,0:T(8,128)(2,1)} %wq_hbm.1, bf16[64,2048]{1,0:T(8,128)(2,1)} %wk_hbm.1, bf16[64,2048]{1,0:T(8,128)(2,1)} %wv_hbm.1, bf16[2048,512]{1,0:T(8,128)(2,1)} %wo_hbm.1, f32[1,2048]{1,0:T(1,128)} %bitcast.5, ...), custom_call_target="tpu_custom_call" | custom-call | tf_op jit(solution)/shard_map/pallas_call | solution.py:666
  65.5 1.5 %copy.16 = bf16[1,16,2048]{2,1,0:T(8,128)(2,1)} copy(bf16[1,16,2048]{2,1,0:T(8,128)(2,1)} %shard_map.136) | data formatting | bytes 131072

commit v4 on v2

--- a/solution.py
+++ b/solution.py
@@ -577,31 +577,36 @@
             partial[h, py, px].astype(f32) + from_core[py, px].astype(f32)
         ).astype(bf16)
 
+    def diag_send(k):
+        send(f"bd{k}", partial.at[h, oy, ox, flip(z, k)], from_diag.at[k], "x" if k % 2 else "y")
+
+    def side_send(way, k, after_diag):
+        py, px = (y, ox) if way == "x" else (oy, x)
+        zk = flip(z, k)
+        if after_diag:
+            arrive(f"bd{k}", from_diag.at[k], "x" if k % 2 else "y")
+            partial[h, py, px, zk] = (
+                partial[h, py, px, zk].astype(f32) + from_diag[k].astype(f32)
+            ).astype(bf16)
+        there = from_x if way == "x" else from_y
+        send(f"b{way}{k}", partial.at[h, py, px, zk], there.at[k], way)
+
+    join("d", oy, ox)
+    diag_send(3)
+    diag_send(2)
     join("x", y, ox)
-    join("d", oy, ox)
-    for k in range(4):
-        zk = flip(z, k)
-        send(f"bd{k}", partial.at[h, oy, ox, zk], from_diag.at[k], "x" if k < 2 else "y")
-    for k in (1, 0):
-        send(f"bx{k}", partial.at[h, y, ox, flip(z, k)], from_x.at[k], "x")
+    side_send("x", 3, False)
     join("y", oy, x)
-    for k in (3, 2):
-        send(f"by{k}", partial.at[h, oy, x, flip(z, k)], from_y.at[k], "y")
+    side_send("y", 2, False)
+    side_send("y", 3, True)
+    side_send("x", 2, True)
+    diag_send(1)
+    diag_send(0)
+    side_send("x", 1, False)
     join("o", y, x)
-    for k in (3, 2):
-        zk = flip(z, k)
-        arrive(f"bd{k}", from_diag.at[k], "y")
-        partial[h, y, ox, zk] = (
-            partial[h, y, ox, zk].astype(f32) + from_diag[k].astype(f32)
-        ).astype(bf16)
-        send(f"bx{k}", partial.at[h, y, ox, zk], from_x.at[k], "x")
-    for k in (1, 0):
-        zk = flip(z, k)
-        arrive(f"bd{k}", from_diag.at[k], "x")
-        partial[h, oy, x, zk] = (
-            partial[h, oy, x, zk].astype(f32) + from_diag[k].astype(f32)
-        ).astype(bf16)
-        send(f"by{k}", partial.at[h, oy, x, zk], from_y.at[k], "y")
+    side_send("y", 1, True)
+    side_send("y", 0, False)
+    side_send("x", 0, True)
     result = None
     for k in (3, 2, 1, 0):
         zk = flip(z, k)

time: 65.9 us -> 66.1 us (level)
  no operation moved by 1% of the time
where the time goes in v4:
time: 66.1 us; the launch traced here: 66 us
  Pallas kernels  64.5 us (98%)
  local copies, waits for them, and re-layouts  1.47 us (2%)
    pallas_call x1, Pallas kernels, fused(): pl.pallas_call(functools.partial(layer_kernel, ctxs * heads), out_shape=j...  64.5 us
    unnamed x1, local copies, waits for them, and re-layouts  1.47 us

profile of v4, /device:TPU:0, one launch (start us, length us, event | category | flops | bytes accessed | tf_op | source)
XLA Modules:
  0.0 66.0 jit_solution(11584270617993884205)
XLA Ops:
  0.0 64.5 %shard_map.136 = bf16[1,16,2048]{2,1,0:T(8,128)(2,1)} custom-call(bf16[2,16,2048]{2,1,0:T(8,128)(2,1)} %tokens_hbm.1, f32[1,2048]{1,0:T(1,128)} %bitcast.4, bf16[2048,512]{1,0:T(8,128)(2,1)} %wq_hbm.1, bf16[64,2048]{1,0:T(8,128)(2,1)} %wk_hbm.1, bf16[64,2048]{1,0:T(8,128)(2,1)} %wv_hbm.1, bf16[2048,512]{1,0:T(8,128)(2,1)} %wo_hbm.1, f32[1,2048]{1,0:T(1,128)} %bitcast.5, ...), custom_call_target="tpu_custom_call" | custom-call | tf_op jit(solution)/shard_map/pallas_call | solution.py:659
  64.5 1.5 %copy.16 = bf16[1,16,2048]{2,1,0:T(8,128)(2,1)} copy(bf16[1,16,2048]{2,1,0:T(8,128)(2,1)} %shard_map.136) | data formatting | bytes 131072
